TPU v7x, 32 devices: a whole 2x2x4 slice. The times are simulated.
32 devices in a mesh: shot: 2 (over y), gx: 16 (over z, x, core).
Axes of the slice: x: 2, y: 2, z: 4, core: 2. Of those that a mesh axis runs over, the one named last changes fastest.
Arguments:
- wave_now: float32 [4, 256, 16, 256], P('shot', 'gx'), parts along dimension 0, may hold values from -18 to 18
- wave_prev: float32 [4, 256, 16, 256], P('shot', 'gx'), parts along dimension 0, may hold values from -18 to 18
- courant: float32 [256, 32, 256], P('gx', 'shot'), parts along dimension 1, may hold values from 0.09 to 0.17
- epsilon: float32 [256, 32, 256], P('gx', 'shot'), parts along dimension 1, may hold values from 0.15 to 0.3
- tilt: float32 [256, 32, 256], P('gx', 'shot'), parts along dimension 1, may hold values from -0.5 to 0.5
- trace_index: int32 [256, 512], P('gx', 'shot'), parts along dimension 1, may hold values from 0 to 2047
- traces: float32 [32, 2048], P('shot'), parts along dimension 0, may hold values from -6 to 6
- lag_list: int32 [33], replicated, may hold values from 0 to 32, each once
Outputs:
- image_out: bfloat16 [66, 256, 16, 256], P('shot', 'gx'), parts along dimension 0
- wave_out: float32 [4, 256, 16, 256], P('shot', 'gx'), parts along dimension 0
There are 2 independent parts, one for each index of `shot`. A program takes and returns all parts, laid end to end along the dimension named above; an argument that names none is the same for every part. Nothing has to cross between parts.
Inputs may be any that keep to these rules, and one draw needn't show every extreme that they name: Each of 0 to 32 once; entry k selects offset lag_list[k] - 16.
All inputs are finite; a program needn't handle non-finite values.
Results may differ from a plain program's by a relative error of at most 0.0058.
Values may be sent and summed in bfloat16 or wider, within the bound.
A program may use at most 128 MiB of HBM per device.

v0:
```python
import jax
import jax.numpy as jnp
from jax import lax
from jax.sharding import PartitionSpec as P

SUB = 4
SNAPS = 4
LAGS = 33
HALF = 16


CENTER = -2.5
NEAR = 4.0 / 3.0
FAR = -1.0 / 12.0


def with_halo(block, sides, width):
    for axis, dim in sides:
        count = lax.axis_size(axis)
        forward = [(i, i + 1) for i in range(count - 1)]
        backward = [(target, source) for source, target in forward]
        low = lax.ppermute(
            lax.slice_in_dim(block, block.shape[dim] - width, None, axis=dim), axis, forward
        )
        high = lax.ppermute(lax.slice_in_dim(block, 0, width, axis=dim), axis, backward)
        block = jnp.concatenate([low, block, high], axis=dim)
    return block


def coefficients(epsilon, tilt):
    cosine_tilt = jnp.cos(tilt)
    sine_tilt = jnp.sin(tilt)
    stretch = 1.0 + 2.0 * epsilon
    coef_a = stretch * cosine_tilt * cosine_tilt + sine_tilt * sine_tilt
    coef_b = stretch * sine_tilt * sine_tilt + cosine_tilt * cosine_tilt
    coef_c = 2.0 * epsilon * jnp.sin(2.0 * tilt)
    return (coef_a, coef_b, coef_c)


def operator(extended, coef_a, coef_b, coef_c):
    length_out = extended.shape[1] - 4
    depth_cells = extended.shape[2]
    cross_cells = extended.shape[3]
    padded = jnp.pad(extended, ((0, 0), (0, 0), (2, 2), (2, 2)))

    def shifted(move_x, move_z, move_y):
        return padded[
            :,
            2 + move_x : 2 + move_x + length_out,
            2 + move_z : 2 + move_z + depth_cells,
            2 + move_y : 2 + move_y + cross_cells,
        ]

    middle = shifted(0, 0, 0)
    second_x = (
        CENTER * middle
        + NEAR * (shifted(1, 0, 0) + shifted(-1, 0, 0))
        + FAR * (shifted(2, 0, 0) + shifted(-2, 0, 0))
    )
    second_z = (
        CENTER * middle
        + NEAR * (shifted(0, 1, 0) + shifted(0, -1, 0))
        + FAR * (shifted(0, 2, 0) + shifted(0, -2, 0))
    )
    second_y = (
        CENTER * middle
        + NEAR * (shifted(0, 0, 1) + shifted(0, 0, -1))
        + FAR * (shifted(0, 0, 2) + shifted(0, 0, -2))
    )
    mixed = 0.25 * (shifted(1, 1, 0) - shifted(1, -1, 0) - shifted(-1, 1, 0) + shifted(-1, -1, 0))
    return coef_a * second_x + coef_b * second_z + second_y + coef_c * mixed


def correlate(extended, slab_width):
    products = []
    for offset in range(-HALF, HALF + 1):
        source = extended[0, HALF - offset : HALF - offset + slab_width]
        receiver = extended[1, HALF + offset : HALF + offset + slab_width]
        products.append(source.astype(jnp.float32) * receiver.astype(jnp.float32))
    return jnp.stack(products)


def body(wave_now, wave_prev, courant, epsilon, tilt, trace_index, traces, lag_list):
    coef_a, coef_b, coef_c = coefficients(epsilon, tilt)
    inject = traces[:, trace_index]
    slab_width = wave_now.shape[1]
    image_zero = jnp.zeros((LAGS, slab_width, wave_now.shape[2], wave_now.shape[3]), jnp.float32)

    def block_pass(block_index, carried):
        current, previous, image_sum = carried
        snapshot = current.astype(jnp.bfloat16)
        extended = with_halo(snapshot, (("gx", 1),), HALF)
        image_sum = image_sum + correlate(extended, slab_width)
        for substep in range(SUB):
            beside_all = with_halo(current, (("gx", 1),), 2)
            advanced = (
                2.0 * current - previous + courant * operator(beside_all, coef_a, coef_b, coef_c)
            )
            source_row = lax.dynamic_index_in_dim(
                inject, block_index * SUB + substep, 0, keepdims=False
            )
            advanced = advanced.at[1, :, 0, :].add(source_row)
            previous, current = (current, advanced)
        return (current, previous, image_sum)

    current, previous, image_sum = lax.fori_loop(
        0, SNAPS, block_pass, (wave_now, wave_prev, image_zero)
    )
    image_out = jnp.take(image_sum, lag_list, axis=0).astype(jnp.bfloat16)
    return (image_out, current)


def solution(mesh):
    placed = (
        P("shot", "gx", None, None),
        P("shot", "gx", None, None),
        P("gx", "shot", None),
        P("gx", "shot", None),
        P("gx", "shot", None),
        P("gx", "shot"),
        P("shot", None),
        P(),
    )
    return jax.shard_map(
        body,
        mesh=mesh,
        in_specs=placed,
        out_specs=(P("shot", "gx", None, None), P("shot", "gx", None, None)),
        check_vma=False,
    )
```

profile of v0, /device:TPU:1, one launch (start us, length us, event | category | flops | bytes accessed | tf_op | source)
XLA Modules:
  0.0 322.7 jit_solution(2500445046619120807)
XLA Ops:
  7.6 15.4 %gather_fusion = f32[4096,16]{1,0:T(8,128)} fusion(f32[16,2048]{0,1:T(8,128)} %copy.12, s32[4096]{0:T(1024)S(1)} %broadcast_clamp_fusion), kind=kCustom, calls=%fused_computation | custom fusion | bytes 540672 | tf_op jit(solution)/shard_map/gather | solution.py:85
  25.9 282.3 %while.24 = (s32[]{:T(128)}, f32[2,16,16,256]{3,2,1,0:T(8,128)S(1)}, f32[2,16,16,256]{3,2,1,0:T(8,128)S(1)}, f32[33,16,16,256]{3,2,1,0:T(8,128)}, f32[16,16,256]...) while((s32[]{:T(128)}, ...), condition=%wide.region_1.2_spmd.clone, body=%wide.region_0.1_spmd.clone.sunk | while | flops 53653000 | bytes 147966848 | solution.py:106
  27.9 4.5 %collective-permute-start.1 = (f32[2,2,16,256]{3,2,1,0:T(8,128)S(1)}, f32[2,2,16,256]{3,2,1,0:T(8,128)S(1)}, u32[]{:S(2)}, u32[]{:S(2)}) collective-permute-start(f32[2,2,16,256]{3,2,1,0:T(8,128)S(1)} %get-tuple-element.449), channel_id=1, source_target_pairs={{0,1},{1,2},{2,3},{3,4},{4,5},{5,6},{6,7},{7,8},{8,9},{9,10},{10,1... | collective-permute-start | bytes 196616 | tf_op jit(solution)/shard_map/while/body/eval_jaxpr/ppermute | solution.py:22
  37.0 4.3 %collective-permute-start.2 = (f32[2,2,16,256]{3,2,1,0:T(8,128)S(1)}, f32[2,2,16,256]{3,2,1,0:T(8,128)S(1)}, u32[]{:S(2)}, u32[]{:S(2)}) collective-permute-start(f32[2,2,16,256]{3,2,1,0:T(8,128)S(1)} %get-tuple-element.452), channel_id=1, source_target_pairs={{0,1},{1,2},{2,3},{3,4},{4,5},{5,6},{6,7},{7,8},{8,9},{9,10},{10,1... | collective-permute-start | bytes 196616 | tf_op jit(solution)/shard_map/while/body/eval_jaxpr/ppermute | solution.py:22
  43.3 3.6 %collective-permute-done.3 = f32[2,2,16,256]{3,2,1,0:T(8,128)S(1)} collective-permute-done((f32[2,2,16,256]{3,2,1,0:T(8,128)S(1)}, f32[2,2,16,256]{3,2,1,0:T(8,128)S(1)}, u32[]{:S(2)}, u32[]{:S(2)}) %collective-permute-start.3) | collective-permute-done | bytes 65568 | tf_op jit(solution)/shard_map/while/body/eval_jaxpr/ppermute | solution.py:25
  54.4 5.7 %collective-permute-done.5 = f32[2,2,16,256]{3,2,1,0:T(8,128)S(1)} collective-permute-done((f32[2,2,16,256]{3,2,1,0:T(8,128)S(1)}, f32[2,2,16,256]{3,2,1,0:T(8,128)S(1)}, u32[]{:S(2)}, u32[]{:S(2)}) %collective-permute-start.5) | collective-permute-done | bytes 65568 | tf_op jit(solution)/shard_map/while/body/eval_jaxpr/ppermute | solution.py:25
  67.6 4.1 %collective-permute-start.8 = (bf16[2,16,16,256]{3,2,1,0:T(8,128)(2,1)S(1)}, bf16[2,16,16,256]{3,2,1,0:T(8,128)(2,1)S(1)}, u32[]{:S(2)}, u32[]{:S(2)}) collective-permute-start(bf16[2,16,16,256]{3,2,1,0:T(8,128)(2,1)S(1)} %get-tuple-element.458), channel_id=1, source_target_pairs={{0,1},{1,2},{2,3},{3,4},{4,5},{5,6},{6,7},{7,8},{8,9},{9,10},{10,1... | collective-permute-start | bytes 786440 | tf_op jit(solution)/shard_map/while/body/eval_jaxpr/ppermute | solution.py:22
  80.7 3.4 %copy-done.2 = f32[33,16,16,256]{3,2,1,0:T(8,128)} copy-done((f32[33,16,16,256]{3,2,1,0:T(8,128)}, f32[33,16,16,256]{3,2,1,0:T(8,128)S(1)}, u32[]{:S(2)}) %copy-start.2) | copy-done | bytes 8650776 | tf_op jit(solution)/shard_map/while
  84.0 9.8 %select_add_fusion.2 = f32[33,16,16,256]{3,2,1,0:T(8,128)} fusion(f32[33,16,16,256]{3,2,1,0:T(8,128)} %copy-done.2, f32[33,16,16,256]{3,2,1,0:T(8,128)} %get-tuple-element.480, pred[]{:T(512)S(6)} %compare.198), kind=kLoop, calls=%fused_computation.2.clone.1 | loop fusion | flops 4325376 | bytes 25952256 | tf_op jit(solution)/shard_map/while/body/eval_jaxpr/add | solution.py:93
  95.8 3.6 %collective-permute-start.1 = (f32[2,2,16,256]{3,2,1,0:T(8,128)S(1)}, f32[2,2,16,256]{3,2,1,0:T(8,128)S(1)}, u32[]{:S(2)}, u32[]{:S(2)}) collective-permute-start(f32[2,2,16,256]{3,2,1,0:T(8,128)S(1)} %get-tuple-element.449), channel_id=1, source_target_pairs={{0,1},{1,2},{2,3},{3,4},{4,5},{5,6},{6,7},{7,8},{8,9},{9,10},{10,1... | collective-permute-start | bytes 196616 | tf_op jit(solution)/shard_map/while/body/eval_jaxpr/ppermute | solution.py:22
  104.1 4.3 %collective-permute-start.2 = (f32[2,2,16,256]{3,2,1,0:T(8,128)S(1)}, f32[2,2,16,256]{3,2,1,0:T(8,128)S(1)}, u32[]{:S(2)}, u32[]{:S(2)}) collective-permute-start(f32[2,2,16,256]{3,2,1,0:T(8,128)S(1)} %get-tuple-element.452), channel_id=1, source_target_pairs={{0,1},{1,2},{2,3},{3,4},{4,5},{5,6},{6,7},{7,8},{8,9},{9,10},{10,1... | collective-permute-start | bytes 196616 | tf_op jit(solution)/shard_map/while/body/eval_jaxpr/ppermute | solution.py:22
  110.3 4.0 %collective-permute-done.3 = f32[2,2,16,256]{3,2,1,0:T(8,128)S(1)} collective-permute-done((f32[2,2,16,256]{3,2,1,0:T(8,128)S(1)}, f32[2,2,16,256]{3,2,1,0:T(8,128)S(1)}, u32[]{:S(2)}, u32[]{:S(2)}) %collective-permute-start.3) | collective-permute-done | bytes 65568 | tf_op jit(solution)/shard_map/while/body/eval_jaxpr/ppermute | solution.py:25
  117.5 4.0 %collective-permute-start.4 = (f32[2,2,16,256]{3,2,1,0:T(8,128)S(1)}, f32[2,2,16,256]{3,2,1,0:T(8,128)S(1)}, u32[]{:S(2)}, u32[]{:S(2)}) collective-permute-start(f32[2,2,16,256]{3,2,1,0:T(8,128)S(1)} %get-tuple-element.454), channel_id=1, source_target_pairs={{0,1},{1,2},{2,3},{3,4},{4,5},{5,6},{6,7},{7,8},{8,9},{9,10},{10,1... | collective-permute-start | bytes 196616 | tf_op jit(solution)/shard_map/while/body/eval_jaxpr/ppermute | solution.py:22
  123.4 5.7 %collective-permute-done.5 = f32[2,2,16,256]{3,2,1,0:T(8,128)S(1)} collective-permute-done((f32[2,2,16,256]{3,2,1,0:T(8,128)S(1)}, f32[2,2,16,256]{3,2,1,0:T(8,128)S(1)}, u32[]{:S(2)}, u32[]{:S(2)}) %collective-permute-start.5) | collective-permute-done | bytes 65568 | tf_op jit(solution)/shard_map/while/body/eval_jaxpr/ppermute | solution.py:25
  136.6 4.1 %collective-permute-start.8 = (bf16[2,16,16,256]{3,2,1,0:T(8,128)(2,1)S(1)}, bf16[2,16,16,256]{3,2,1,0:T(8,128)(2,1)S(1)}, u32[]{:S(2)}, u32[]{:S(2)}) collective-permute-start(bf16[2,16,16,256]{3,2,1,0:T(8,128)(2,1)S(1)} %get-tuple-element.458), channel_id=1, source_target_pairs={{0,1},{1,2},{2,3},{3,4},{4,5},{5,6},{6,7},{7,8},{8,9},{9,10},{10,1... | collective-permute-start | bytes 786440 | tf_op jit(solution)/shard_map/while/body/eval_jaxpr/ppermute | solution.py:22
  153.0 12.2 %select_add_fusion.2 = f32[33,16,16,256]{3,2,1,0:T(8,128)} fusion(f32[33,16,16,256]{3,2,1,0:T(8,128)} %copy-done.2, f32[33,16,16,256]{3,2,1,0:T(8,128)} %get-tuple-element.480, pred[]{:T(512)S(6)} %compare.198), kind=kLoop, calls=%fused_computation.2.clone.1 | loop fusion | flops 4325376 | bytes 25952256 | tf_op jit(solution)/shard_map/while/body/eval_jaxpr/add | solution.py:93
  167.2 3.6 %collective-permute-start.1 = (f32[2,2,16,256]{3,2,1,0:T(8,128)S(1)}, f32[2,2,16,256]{3,2,1,0:T(8,128)S(1)}, u32[]{:S(2)}, u32[]{:S(2)}) collective-permute-start(f32[2,2,16,256]{3,2,1,0:T(8,128)S(1)} %get-tuple-element.449), channel_id=1, source_target_pairs={{0,1},{1,2},{2,3},{3,4},{4,5},{5,6},{6,7},{7,8},{8,9},{9,10},{10,1... | collective-permute-start | bytes 196616 | tf_op jit(solution)/shard_map/while/body/eval_jaxpr/ppermute | solution.py:22
  175.5 4.3 %collective-permute-start.2 = (f32[2,2,16,256]{3,2,1,0:T(8,128)S(1)}, f32[2,2,16,256]{3,2,1,0:T(8,128)S(1)}, u32[]{:S(2)}, u32[]{:S(2)}) collective-permute-start(f32[2,2,16,256]{3,2,1,0:T(8,128)S(1)} %get-tuple-element.452), channel_id=1, source_target_pairs={{0,1},{1,2},{2,3},{3,4},{4,5},{5,6},{6,7},{7,8},{8,9},{9,10},{10,1... | collective-permute-start | bytes 196616 | tf_op jit(solution)/shard_map/while/body/eval_jaxpr/ppermute | solution.py:22
  181.7 4.0 %collective-permute-done.3 = f32[2,2,16,256]{3,2,1,0:T(8,128)S(1)} collective-permute-done((f32[2,2,16,256]{3,2,1,0:T(8,128)S(1)}, f32[2,2,16,256]{3,2,1,0:T(8,128)S(1)}, u32[]{:S(2)}, u32[]{:S(2)}) %collective-permute-start.3) | collective-permute-done | bytes 65568 | tf_op jit(solution)/shard_map/while/body/eval_jaxpr/ppermute | solution.py:25
  188.9 4.0 %collective-permute-start.4 = (f32[2,2,16,256]{3,2,1,0:T(8,128)S(1)}, f32[2,2,16,256]{3,2,1,0:T(8,128)S(1)}, u32[]{:S(2)}, u32[]{:S(2)}) collective-permute-start(f32[2,2,16,256]{3,2,1,0:T(8,128)S(1)} %get-tuple-element.454), channel_id=1, source_target_pairs={{0,1},{1,2},{2,3},{3,4},{4,5},{5,6},{6,7},{7,8},{8,9},{9,10},{10,1... | collective-permute-start | bytes 196616 | tf_op jit(solution)/shard_map/while/body/eval_jaxpr/ppermute | solution.py:22
  194.8 5.7 %collective-permute-done.5 = f32[2,2,16,256]{3,2,1,0:T(8,128)S(1)} collective-permute-done((f32[2,2,16,256]{3,2,1,0:T(8,128)S(1)}, f32[2,2,16,256]{3,2,1,0:T(8,128)S(1)}, u32[]{:S(2)}, u32[]{:S(2)}) %collective-permute-start.5) | collective-permute-done | bytes 65568 | tf_op jit(solution)/shard_map/while/body/eval_jaxpr/ppermute | solution.py:25
  208.1 4.1 %collective-permute-start.8 = (bf16[2,16,16,256]{3,2,1,0:T(8,128)(2,1)S(1)}, bf16[2,16,16,256]{3,2,1,0:T(8,128)(2,1)S(1)}, u32[]{:S(2)}, u32[]{:S(2)}) collective-permute-start(bf16[2,16,16,256]{3,2,1,0:T(8,128)(2,1)S(1)} %get-tuple-element.458), channel_id=1, source_target_pairs={{0,1},{1,2},{2,3},{3,4},{4,5},{5,6},{6,7},{7,8},{8,9},{9,10},{10,1... | collective-permute-start | bytes 786440 | tf_op jit(solution)/shard_map/while/body/eval_jaxpr/ppermute | solution.py:22
  224.5 12.2 %select_add_fusion.2 = f32[33,16,16,256]{3,2,1,0:T(8,128)} fusion(f32[33,16,16,256]{3,2,1,0:T(8,128)} %copy-done.2, f32[33,16,16,256]{3,2,1,0:T(8,128)} %get-tuple-element.480, pred[]{:T(512)S(6)} %compare.198), kind=kLoop, calls=%fused_computation.2.clone.1 | loop fusion | flops 4325376 | bytes 25952256 | tf_op jit(solution)/shard_map/while/body/eval_jaxpr/add | solution.py:93
  238.7 3.6 %collective-permute-start.1 = (f32[2,2,16,256]{3,2,1,0:T(8,128)S(1)}, f32[2,2,16,256]{3,2,1,0:T(8,128)S(1)}, u32[]{:S(2)}, u32[]{:S(2)}) collective-permute-start(f32[2,2,16,256]{3,2,1,0:T(8,128)S(1)} %get-tuple-element.449), channel_id=1, source_target_pairs={{0,1},{1,2},{2,3},{3,4},{4,5},{5,6},{6,7},{7,8},{8,9},{9,10},{10,1... | collective-permute-start | bytes 196616 | tf_op jit(solution)/shard_map/while/body/eval_jaxpr/ppermute | solution.py:22
  247.0 4.3 %collective-permute-start.2 = (f32[2,2,16,256]{3,2,1,0:T(8,128)S(1)}, f32[2,2,16,256]{3,2,1,0:T(8,128)S(1)}, u32[]{:S(2)}, u32[]{:S(2)}) collective-permute-start(f32[2,2,16,256]{3,2,1,0:T(8,128)S(1)} %get-tuple-element.452), channel_id=1, source_target_pairs={{0,1},{1,2},{2,3},{3,4},{4,5},{5,6},{6,7},{7,8},{8,9},{9,10},{10,1... | collective-permute-start | bytes 196616 | tf_op jit(solution)/shard_map/while/body/eval_jaxpr/ppermute | solution.py:22
  253.2 4.0 %collective-permute-done.3 = f32[2,2,16,256]{3,2,1,0:T(8,128)S(1)} collective-permute-done((f32[2,2,16,256]{3,2,1,0:T(8,128)S(1)}, f32[2,2,16,256]{3,2,1,0:T(8,128)S(1)}, u32[]{:S(2)}, u32[]{:S(2)}) %collective-permute-start.3) | collective-permute-done | bytes 65568 | tf_op jit(solution)/shard_map/while/body/eval_jaxpr/ppermute | solution.py:25
  260.4 4.0 %collective-permute-start.4 = (f32[2,2,16,256]{3,2,1,0:T(8,128)S(1)}, f32[2,2,16,256]{3,2,1,0:T(8,128)S(1)}, u32[]{:S(2)}, u32[]{:S(2)}) collective-permute-start(f32[2,2,16,256]{3,2,1,0:T(8,128)S(1)} %get-tuple-element.454), channel_id=1, source_target_pairs={{0,1},{1,2},{2,3},{3,4},{4,5},{5,6},{6,7},{7,8},{8,9},{9,10},{10,1... | collective-permute-start | bytes 196616 | tf_op jit(solution)/shard_map/while/body/eval_jaxpr/ppermute | solution.py:22
  266.3 5.7 %collective-permute-done.5 = f32[2,2,16,256]{3,2,1,0:T(8,128)S(1)} collective-permute-done((f32[2,2,16,256]{3,2,1,0:T(8,128)S(1)}, f32[2,2,16,256]{3,2,1,0:T(8,128)S(1)}, u32[]{:S(2)}, u32[]{:S(2)}) %collective-permute-start.5) | collective-permute-done | bytes 65568 | tf_op jit(solution)/shard_map/while/body/eval_jaxpr/ppermute | solution.py:25
  279.6 4.1 %collective-permute-start.8 = (bf16[2,16,16,256]{3,2,1,0:T(8,128)(2,1)S(1)}, bf16[2,16,16,256]{3,2,1,0:T(8,128)(2,1)S(1)}, u32[]{:S(2)}, u32[]{:S(2)}) collective-permute-start(bf16[2,16,16,256]{3,2,1,0:T(8,128)(2,1)S(1)} %get-tuple-element.458), channel_id=1, source_target_pairs={{0,1},{1,2},{2,3},{3,4},{4,5},{5,6},{6,7},{7,8},{8,9},{9,10},{10,1... | collective-permute-start | bytes 786440 | tf_op jit(solution)/shard_map/while/body/eval_jaxpr/ppermute | solution.py:22
  296.0 12.2 %select_add_fusion.2 = f32[33,16,16,256]{3,2,1,0:T(8,128)} fusion(f32[33,16,16,256]{3,2,1,0:T(8,128)} %copy-done.2, f32[33,16,16,256]{3,2,1,0:T(8,128)} %get-tuple-element.480, pred[]{:T(512)S(6)} %compare.198), kind=kLoop, calls=%fused_computation.2.clone.1 | loop fusion | flops 4325376 | bytes 25952256 | tf_op jit(solution)/shard_map/while/body/eval_jaxpr/add | solution.py:93
  308.2 8.6 %gather_fusion.1 = bf16[33,16,16,256]{3,2,1,0:T(8,128)(2,1)} fusion(f32[33,16,16,256]{3,2,1,0:T(8,128)} %get-tuple-element.316, s32[1024]{0:T(1024)S(1)} %pad_clamp_fusion), kind=kCustom, calls=%fused_computation.1 | custom fusion | bytes 8650884 | tf_op jit(solution)/shard_map/jit(_take)/gather | solution.py:109
  316.8 5.8 %select_convert_fusion = bf16[33,16,16,256]{3,2,1,0:T(8,128)(2,1)} fusion(bf16[33,16,16,256]{3,2,1,0:T(8,128)(2,1)} %gather_fusion.1, pred[33]{0:T(512)(128)(4,1)S(1)} %compare_and_fusion), kind=kLoop, calls=%fused_computation.376 | loop fusion | flops 2162688 | bytes 8650785 | tf_op jit(solution)/shard_map/convert_element_type | solution.py:109
  (329 shorter events, 140.9 us)
Async XLA Ops:
  25.9 7.9 %collective-permute-start = (f32[2,2,16,256]{3,2,1,0:T(8,128)S(1)}, f32[2,2,16,256]{3,2,1,0:T(8,128)S(1)}, u32[]{:S(2)}, u32[]{:S(2)}) collective-permute-start(f32[2,2,16,256]{3,2,1,0:T(8,128)S(1)} %get-tuple-element.448), channel_id=1, source_target_pairs={{1,0},{2,1},{3,2},{4,3},{5,4},{6,5},{7,6},{8,7},{9,8},{10,9},{11,1... | collective-permute-start | bytes 196616 | tf_op jit(solution)/shard_map/while/body/eval_jaxpr/ppermute | solution.py:25
  37.0 6.2 %collective-permute-start.2 = (f32[2,2,16,256]{3,2,1,0:T(8,128)S(1)}, f32[2,2,16,256]{3,2,1,0:T(8,128)S(1)}, u32[]{:S(2)}, u32[]{:S(2)}) collective-permute-start(f32[2,2,16,256]{3,2,1,0:T(8,128)S(1)} %get-tuple-element.452), channel_id=1, source_target_pairs={{0,1},{1,2},{2,3},{3,4},{4,5},{5,6},{6,7},{7,8},{8,9},{9,10},{10,1... | collective-permute-start | bytes 196616 | tf_op jit(solution)/shard_map/while/body/eval_jaxpr/ppermute | solution.py:22
  52.4 7.7 %collective-permute-start.5 = (f32[2,2,16,256]{3,2,1,0:T(8,128)S(1)}, f32[2,2,16,256]{3,2,1,0:T(8,128)S(1)}, u32[]{:S(2)}, u32[]{:S(2)}) collective-permute-start(f32[2,2,16,256]{3,2,1,0:T(8,128)S(1)} %get-tuple-element.455), channel_id=1, source_target_pairs={{1,0},{2,1},{3,2},{4,3},{5,4},{6,5},{7,6},{8,7},{9,8},{10,9},{11,1... | collective-permute-start | bytes 196616 | tf_op jit(solution)/shard_map/while/body/eval_jaxpr/ppermute | solution.py:25
  63.3 10.4 %collective-permute-start.6 = (f32[2,2,16,256]{3,2,1,0:T(8,128)S(1)}, f32[2,2,16,256]{3,2,1,0:T(8,128)S(1)}, u32[]{:S(2)}, u32[]{:S(2)}) collective-permute-start(f32[2,2,16,256]{3,2,1,0:T(8,128)S(1)} %get-tuple-element.456), channel_id=1, source_target_pairs={{0,1},{1,2},{2,3},{3,4},{4,5},{5,6},{6,7},{7,8},{8,9},{9,10},{10,1... | collective-permute-start | bytes 196616 | tf_op jit(solution)/shard_map/while/body/eval_jaxpr/ppermute | solution.py:22
  65.2 8.4 %collective-permute-start.7 = (f32[2,2,16,256]{3,2,1,0:T(8,128)S(1)}, f32[2,2,16,256]{3,2,1,0:T(8,128)S(1)}, u32[]{:S(2)}, u32[]{:S(2)}) collective-permute-start(f32[2,2,16,256]{3,2,1,0:T(8,128)S(1)} %get-tuple-element.457), channel_id=1, source_target_pairs={{1,0},{2,1},{3,2},{4,3},{5,4},{6,5},{7,6},{8,7},{9,8},{10,9},{11,1... | collective-permute-start | bytes 196616 | tf_op jit(solution)/shard_map/while/body/eval_jaxpr/ppermute | solution.py:25
  67.6 9.2 %collective-permute-start.8 = (bf16[2,16,16,256]{3,2,1,0:T(8,128)(2,1)S(1)}, bf16[2,16,16,256]{3,2,1,0:T(8,128)(2,1)S(1)}, u32[]{:S(2)}, u32[]{:S(2)}) collective-permute-start(bf16[2,16,16,256]{3,2,1,0:T(8,128)(2,1)S(1)} %get-tuple-element.458), channel_id=1, source_target_pairs={{0,1},{1,2},{2,3},{3,4},{4,5},{5,6},{6,7},{7,8},{8,9},{9,10},{10,1... | collective-permute-start | bytes 786440 | tf_op jit(solution)/shard_map/while/body/eval_jaxpr/ppermute | solution.py:22
  71.7 7.7 %collective-permute-start.9 = (bf16[2,16,16,256]{3,2,1,0:T(8,128)(2,1)S(1)}, bf16[2,16,16,256]{3,2,1,0:T(8,128)(2,1)S(1)}, u32[]{:S(2)}, u32[]{:S(2)}) collective-permute-start(bf16[2,16,16,256]{3,2,1,0:T(8,128)(2,1)S(1)} %get-tuple-element.458), channel_id=1, source_target_pairs={{1,0},{2,1},{3,2},{4,3},{5,4},{6,5},{7,6},{8,7},{9,8},{10,9},{11,1... | collective-permute-start | bytes 786440 | tf_op jit(solution)/shard_map/while/body/eval_jaxpr/ppermute | solution.py:25
  93.8 7.1 %collective-permute-start = (f32[2,2,16,256]{3,2,1,0:T(8,128)S(1)}, f32[2,2,16,256]{3,2,1,0:T(8,128)S(1)}, u32[]{:S(2)}, u32[]{:S(2)}) collective-permute-start(f32[2,2,16,256]{3,2,1,0:T(8,128)S(1)} %get-tuple-element.448), channel_id=1, source_target_pairs={{1,0},{2,1},{3,2},{4,3},{5,4},{6,5},{7,6},{8,7},{9,8},{10,9},{11,1... | collective-permute-start | bytes 196616 | tf_op jit(solution)/shard_map/while/body/eval_jaxpr/ppermute | solution.py:25
  104.1 6.2 %collective-permute-start.2 = (f32[2,2,16,256]{3,2,1,0:T(8,128)S(1)}, f32[2,2,16,256]{3,2,1,0:T(8,128)S(1)}, u32[]{:S(2)}, u32[]{:S(2)}) collective-permute-start(f32[2,2,16,256]{3,2,1,0:T(8,128)S(1)} %get-tuple-element.452), channel_id=1, source_target_pairs={{0,1},{1,2},{2,3},{3,4},{4,5},{5,6},{6,7},{7,8},{8,9},{9,10},{10,1... | collective-permute-start | bytes 196616 | tf_op jit(solution)/shard_map/while/body/eval_jaxpr/ppermute | solution.py:22
  108.3 5.9 %collective-permute-start.3 = (f32[2,2,16,256]{3,2,1,0:T(8,128)S(1)}, f32[2,2,16,256]{3,2,1,0:T(8,128)S(1)}, u32[]{:S(2)}, u32[]{:S(2)}) collective-permute-start(f32[2,2,16,256]{3,2,1,0:T(8,128)S(1)} %get-tuple-element.453), channel_id=1, source_target_pairs={{1,0},{2,1},{3,2},{4,3},{5,4},{6,5},{7,6},{8,7},{9,8},{10,9},{11,1... | collective-permute-start | bytes 196616 | tf_op jit(solution)/shard_map/while/body/eval_jaxpr/ppermute | solution.py:25
  117.5 5.9 %collective-permute-start.4 = (f32[2,2,16,256]{3,2,1,0:T(8,128)S(1)}, f32[2,2,16,256]{3,2,1,0:T(8,128)S(1)}, u32[]{:S(2)}, u32[]{:S(2)}) collective-permute-start(f32[2,2,16,256]{3,2,1,0:T(8,128)S(1)} %get-tuple-element.454), channel_id=1, source_target_pairs={{0,1},{1,2},{2,3},{3,4},{4,5},{5,6},{6,7},{7,8},{8,9},{9,10},{10,1... | collective-permute-start | bytes 196616 | tf_op jit(solution)/shard_map/while/body/eval_jaxpr/ppermute | solution.py:22
  121.4 7.7 %collective-permute-start.5 = (f32[2,2,16,256]{3,2,1,0:T(8,128)S(1)}, f32[2,2,16,256]{3,2,1,0:T(8,128)S(1)}, u32[]{:S(2)}, u32[]{:S(2)}) collective-permute-start(f32[2,2,16,256]{3,2,1,0:T(8,128)S(1)} %get-tuple-element.455), channel_id=1, source_target_pairs={{1,0},{2,1},{3,2},{4,3},{5,4},{6,5},{7,6},{8,7},{9,8},{10,9},{11,1... | collective-permute-start | bytes 196616 | tf_op jit(solution)/shard_map/while/body/eval_jaxpr/ppermute | solution.py:25
  132.3 10.4 %collective-permute-start.6 = (f32[2,2,16,256]{3,2,1,0:T(8,128)S(1)}, f32[2,2,16,256]{3,2,1,0:T(8,128)S(1)}, u32[]{:S(2)}, u32[]{:S(2)}) collective-permute-start(f32[2,2,16,256]{3,2,1,0:T(8,128)S(1)} %get-tuple-element.456), channel_id=1, source_target_pairs={{0,1},{1,2},{2,3},{3,4},{4,5},{5,6},{6,7},{7,8},{8,9},{9,10},{10,1... | collective-permute-start | bytes 196616 | tf_op jit(solution)/shard_map/while/body/eval_jaxpr/ppermute | solution.py:22
  134.2 8.4 %collective-permute-start.7 = (f32[2,2,16,256]{3,2,1,0:T(8,128)S(1)}, f32[2,2,16,256]{3,2,1,0:T(8,128)S(1)}, u32[]{:S(2)}, u32[]{:S(2)}) collective-permute-start(f32[2,2,16,256]{3,2,1,0:T(8,128)S(1)} %get-tuple-element.457), channel_id=1, source_target_pairs={{1,0},{2,1},{3,2},{4,3},{5,4},{6,5},{7,6},{8,7},{9,8},{10,9},{11,1... | collective-permute-start | bytes 196616 | tf_op jit(solution)/shard_map/while/body/eval_jaxpr/ppermute | solution.py:25
  136.6 9.2 %collective-permute-start.8 = (bf16[2,16,16,256]{3,2,1,0:T(8,128)(2,1)S(1)}, bf16[2,16,16,256]{3,2,1,0:T(8,128)(2,1)S(1)}, u32[]{:S(2)}, u32[]{:S(2)}) collective-permute-start(bf16[2,16,16,256]{3,2,1,0:T(8,128)(2,1)S(1)} %get-tuple-element.458), channel_id=1, source_target_pairs={{0,1},{1,2},{2,3},{3,4},{4,5},{5,6},{6,7},{7,8},{8,9},{9,10},{10,1... | collective-permute-start | bytes 786440 | tf_op jit(solution)/shard_map/while/body/eval_jaxpr/ppermute | solution.py:22
  140.7 7.7 %collective-permute-start.9 = (bf16[2,16,16,256]{3,2,1,0:T(8,128)(2,1)S(1)}, bf16[2,16,16,256]{3,2,1,0:T(8,128)(2,1)S(1)}, u32[]{:S(2)}, u32[]{:S(2)}) collective-permute-start(bf16[2,16,16,256]{3,2,1,0:T(8,128)(2,1)S(1)} %get-tuple-element.458), channel_id=1, source_target_pairs={{1,0},{2,1},{3,2},{4,3},{5,4},{6,5},{7,6},{8,7},{9,8},{10,9},{11,1... | collective-permute-start | bytes 786440 | tf_op jit(solution)/shard_map/while/body/eval_jaxpr/ppermute | solution.py:25
  165.3 7.1 %collective-permute-start = (f32[2,2,16,256]{3,2,1,0:T(8,128)S(1)}, f32[2,2,16,256]{3,2,1,0:T(8,128)S(1)}, u32[]{:S(2)}, u32[]{:S(2)}) collective-permute-start(f32[2,2,16,256]{3,2,1,0:T(8,128)S(1)} %get-tuple-element.448), channel_id=1, source_target_pairs={{1,0},{2,1},{3,2},{4,3},{5,4},{6,5},{7,6},{8,7},{9,8},{10,9},{11,1... | collective-permute-start | bytes 196616 | tf_op jit(solution)/shard_map/while/body/eval_jaxpr/ppermute | solution.py:25
  175.5 6.2 %collective-permute-start.2 = (f32[2,2,16,256]{3,2,1,0:T(8,128)S(1)}, f32[2,2,16,256]{3,2,1,0:T(8,128)S(1)}, u32[]{:S(2)}, u32[]{:S(2)}) collective-permute-start(f32[2,2,16,256]{3,2,1,0:T(8,128)S(1)} %get-tuple-element.452), channel_id=1, source_target_pairs={{0,1},{1,2},{2,3},{3,4},{4,5},{5,6},{6,7},{7,8},{8,9},{9,10},{10,1... | collective-permute-start | bytes 196616 | tf_op jit(solution)/shard_map/while/body/eval_jaxpr/ppermute | solution.py:22
  179.8 5.9 %collective-permute-start.3 = (f32[2,2,16,256]{3,2,1,0:T(8,128)S(1)}, f32[2,2,16,256]{3,2,1,0:T(8,128)S(1)}, u32[]{:S(2)}, u32[]{:S(2)}) collective-permute-start(f32[2,2,16,256]{3,2,1,0:T(8,128)S(1)} %get-tuple-element.453), channel_id=1, source_target_pairs={{1,0},{2,1},{3,2},{4,3},{5,4},{6,5},{7,6},{8,7},{9,8},{10,9},{11,1... | collective-permute-start | bytes 196616 | tf_op jit(solution)/shard_map/while/body/eval_jaxpr/ppermute | solution.py:25
  192.9 7.7 %collective-permute-start.5 = (f32[2,2,16,256]{3,2,1,0:T(8,128)S(1)}, f32[2,2,16,256]{3,2,1,0:T(8,128)S(1)}, u32[]{:S(2)}, u32[]{:S(2)}) collective-permute-start(f32[2,2,16,256]{3,2,1,0:T(8,128)S(1)} %get-tuple-element.455), channel_id=1, source_target_pairs={{1,0},{2,1},{3,2},{4,3},{5,4},{6,5},{7,6},{8,7},{9,8},{10,9},{11,1... | collective-permute-start | bytes 196616 | tf_op jit(solution)/shard_map/while/body/eval_jaxpr/ppermute | solution.py:25
  203.8 10.4 %collective-permute-start.6 = (f32[2,2,16,256]{3,2,1,0:T(8,128)S(1)}, f32[2,2,16,256]{3,2,1,0:T(8,128)S(1)}, u32[]{:S(2)}, u32[]{:S(2)}) collective-permute-start(f32[2,2,16,256]{3,2,1,0:T(8,128)S(1)} %get-tuple-element.456), channel_id=1, source_target_pairs={{0,1},{1,2},{2,3},{3,4},{4,5},{5,6},{6,7},{7,8},{8,9},{9,10},{10,1... | collective-permute-start | bytes 196616 | tf_op jit(solution)/shard_map/while/body/eval_jaxpr/ppermute | solution.py:22
  205.7 8.4 %collective-permute-start.7 = (f32[2,2,16,256]{3,2,1,0:T(8,128)S(1)}, f32[2,2,16,256]{3,2,1,0:T(8,128)S(1)}, u32[]{:S(2)}, u32[]{:S(2)}) collective-permute-start(f32[2,2,16,256]{3,2,1,0:T(8,128)S(1)} %get-tuple-element.457), channel_id=1, source_target_pairs={{1,0},{2,1},{3,2},{4,3},{5,4},{6,5},{7,6},{8,7},{9,8},{10,9},{11,1... | collective-permute-start | bytes 196616 | tf_op jit(solution)/shard_map/while/body/eval_jaxpr/ppermute | solution.py:25
  208.1 9.2 %collective-permute-start.8 = (bf16[2,16,16,256]{3,2,1,0:T(8,128)(2,1)S(1)}, bf16[2,16,16,256]{3,2,1,0:T(8,128)(2,1)S(1)}, u32[]{:S(2)}, u32[]{:S(2)}) collective-permute-start(bf16[2,16,16,256]{3,2,1,0:T(8,128)(2,1)S(1)} %get-tuple-element.458), channel_id=1, source_target_pairs={{0,1},{1,2},{2,3},{3,4},{4,5},{5,6},{6,7},{7,8},{8,9},{9,10},{10,1... | collective-permute-start | bytes 786440 | tf_op jit(solution)/shard_map/while/body/eval_jaxpr/ppermute | solution.py:22
  212.2 7.7 %collective-permute-start.9 = (bf16[2,16,16,256]{3,2,1,0:T(8,128)(2,1)S(1)}, bf16[2,16,16,256]{3,2,1,0:T(8,128)(2,1)S(1)}, u32[]{:S(2)}, u32[]{:S(2)}) collective-permute-start(bf16[2,16,16,256]{3,2,1,0:T(8,128)(2,1)S(1)} %get-tuple-element.458), channel_id=1, source_target_pairs={{1,0},{2,1},{3,2},{4,3},{5,4},{6,5},{7,6},{8,7},{9,8},{10,9},{11,1... | collective-permute-start | bytes 786440 | tf_op jit(solution)/shard_map/while/body/eval_jaxpr/ppermute | solution.py:25
  236.8 7.1 %collective-permute-start = (f32[2,2,16,256]{3,2,1,0:T(8,128)S(1)}, f32[2,2,16,256]{3,2,1,0:T(8,128)S(1)}, u32[]{:S(2)}, u32[]{:S(2)}) collective-permute-start(f32[2,2,16,256]{3,2,1,0:T(8,128)S(1)} %get-tuple-element.448), channel_id=1, source_target_pairs={{1,0},{2,1},{3,2},{4,3},{5,4},{6,5},{7,6},{8,7},{9,8},{10,9},{11,1... | collective-permute-start | bytes 196616 | tf_op jit(solution)/shard_map/while/body/eval_jaxpr/ppermute | solution.py:25
  247.0 6.2 %collective-permute-start.2 = (f32[2,2,16,256]{3,2,1,0:T(8,128)S(1)}, f32[2,2,16,256]{3,2,1,0:T(8,128)S(1)}, u32[]{:S(2)}, u32[]{:S(2)}) collective-permute-start(f32[2,2,16,256]{3,2,1,0:T(8,128)S(1)} %get-tuple-element.452), channel_id=1, source_target_pairs={{0,1},{1,2},{2,3},{3,4},{4,5},{5,6},{6,7},{7,8},{8,9},{9,10},{10,1... | collective-permute-start | bytes 196616 | tf_op jit(solution)/shard_map/while/body/eval_jaxpr/ppermute | solution.py:22
  251.3 5.9 %collective-permute-start.3 = (f32[2,2,16,256]{3,2,1,0:T(8,128)S(1)}, f32[2,2,16,256]{3,2,1,0:T(8,128)S(1)}, u32[]{:S(2)}, u32[]{:S(2)}) collective-permute-start(f32[2,2,16,256]{3,2,1,0:T(8,128)S(1)} %get-tuple-element.453), channel_id=1, source_target_pairs={{1,0},{2,1},{3,2},{4,3},{5,4},{6,5},{7,6},{8,7},{9,8},{10,9},{11,1... | collective-permute-start | bytes 196616 | tf_op jit(solution)/shard_map/while/body/eval_jaxpr/ppermute | solution.py:25
  264.4 7.7 %collective-permute-start.5 = (f32[2,2,16,256]{3,2,1,0:T(8,128)S(1)}, f32[2,2,16,256]{3,2,1,0:T(8,128)S(1)}, u32[]{:S(2)}, u32[]{:S(2)}) collective-permute-start(f32[2,2,16,256]{3,2,1,0:T(8,128)S(1)} %get-tuple-element.455), channel_id=1, source_target_pairs={{1,0},{2,1},{3,2},{4,3},{5,4},{6,5},{7,6},{8,7},{9,8},{10,9},{11,1... | collective-permute-start | bytes 196616 | tf_op jit(solution)/shard_map/while/body/eval_jaxpr/ppermute | solution.py:25
  275.2 10.4 %collective-permute-start.6 = (f32[2,2,16,256]{3,2,1,0:T(8,128)S(1)}, f32[2,2,16,256]{3,2,1,0:T(8,128)S(1)}, u32[]{:S(2)}, u32[]{:S(2)}) collective-permute-start(f32[2,2,16,256]{3,2,1,0:T(8,128)S(1)} %get-tuple-element.456), channel_id=1, source_target_pairs={{0,1},{1,2},{2,3},{3,4},{4,5},{5,6},{6,7},{7,8},{8,9},{9,10},{10,1... | collective-permute-start | bytes 196616 | tf_op jit(solution)/shard_map/while/body/eval_jaxpr/ppermute | solution.py:22
  277.1 8.4 %collective-permute-start.7 = (f32[2,2,16,256]{3,2,1,0:T(8,128)S(1)}, f32[2,2,16,256]{3,2,1,0:T(8,128)S(1)}, u32[]{:S(2)}, u32[]{:S(2)}) collective-permute-start(f32[2,2,16,256]{3,2,1,0:T(8,128)S(1)} %get-tuple-element.457), channel_id=1, source_target_pairs={{1,0},{2,1},{3,2},{4,3},{5,4},{6,5},{7,6},{8,7},{9,8},{10,9},{11,1... | collective-permute-start | bytes 196616 | tf_op jit(solution)/shard_map/while/body/eval_jaxpr/ppermute | solution.py:25
  279.6 9.2 %collective-permute-start.8 = (bf16[2,16,16,256]{3,2,1,0:T(8,128)(2,1)S(1)}, bf16[2,16,16,256]{3,2,1,0:T(8,128)(2,1)S(1)}, u32[]{:S(2)}, u32[]{:S(2)}) collective-permute-start(bf16[2,16,16,256]{3,2,1,0:T(8,128)(2,1)S(1)} %get-tuple-element.458), channel_id=1, source_target_pairs={{0,1},{1,2},{2,3},{3,4},{4,5},{5,6},{6,7},{7,8},{8,9},{9,10},{10,1... | collective-permute-start | bytes 786440 | tf_op jit(solution)/shard_map/while/body/eval_jaxpr/ppermute | solution.py:22
  283.6 7.7 %collective-permute-start.9 = (bf16[2,16,16,256]{3,2,1,0:T(8,128)(2,1)S(1)}, bf16[2,16,16,256]{3,2,1,0:T(8,128)(2,1)S(1)}, u32[]{:S(2)}, u32[]{:S(2)}) collective-permute-start(bf16[2,16,16,256]{3,2,1,0:T(8,128)(2,1)S(1)} %get-tuple-element.458), channel_id=1, source_target_pairs={{1,0},{2,1},{3,2},{4,3},{5,4},{6,5},{7,6},{8,7},{9,8},{10,9},{11,1... | collective-permute-start | bytes 786440 | tf_op jit(solution)/shard_map/while/body/eval_jaxpr/ppermute | solution.py:25
  (25 other events, 557.3 us)
where the time goes:
time: 326 us; the launch traced here: 323 us
  starting transfers between devices  111 us (34%)
  other arithmetic  108 us (33%)
  waiting for transfers between devices  53.9 us (17%)
  local copies, waits for them, and re-layouts  46.2 us (14%)
    ppermute x20, starting transfers between devices, with_halo(): lax.ppermute(lax.slice_in_dim(block, block.shape[dim] - width, None, axis...  70.6 us
    ppermute x20, waiting for transfers between devices, with_halo(): lax.ppermute(lax.slice_in_dim(block, 0, width, axis=dim), axis, backward)  48.8 us
    add x4, other arithmetic, block_pass(): image_sum = image_sum + correlate(extended, slab_width)  46.5 us
    ppermute x20, starting transfers between devices, with_halo(): lax.ppermute(lax.slice_in_dim(block, 0, width, axis=dim), axis, backward)  40.5 us
    add x16, other arithmetic, block_pass(): 2.0 * current - previous  26 us
    gather x2, local copies, waits for them, and re-layouts, body(): inject = traces[:, trace_index]  18.3 us
    add x16, other arithmetic, block_pass(): advanced = advanced.at[1, :, 0, :].add(source_row)  14.9 us
    while x28, local copies, waits for them, and re-layouts  13.5 us
  transfers between devices with their start and end apart: 40, of which 16 were waited for; matrix products, arithmetic and copies ran while one was open for 4% of the time, Pallas kernels for 0%

commit v1 on v0

v1 whole, which is shorter than its diff:
```python
import functools

import jax
import jax.numpy as jnp
from jax import lax
from jax.experimental import pallas as pl
from jax.experimental.pallas import tpu as pltpu
from jax.sharding import PartitionSpec as P

SUB = 4
SNAPS = 4
STEPS = 16
LAGS = 33
HALF = 16
MESH = pl.DeviceIdType.MESH
LIMIT = 48 * 1024 * 1024


def prep_kernel(courant, epsilon, tilt, index, traces, coefs, inject):
    def layer(x, carry):
        c = courant[x]
        e2 = 2.0 * epsilon[x]
        s = jnp.sin(tilt[x])
        k = jnp.cos(tilt[x])
        a = c * (1.0 + e2 * k * k)
        b = c * (1.0 + e2 * s * s)
        coefs[0, x] = 2.0 - 2.5 * (a + b + c)
        coefs[1, x] = (4.0 / 3.0) * a
        coefs[2, x] = (4.0 / 3.0) * b
        coefs[3, x] = (4.0 / 3.0) * c
        coefs[4, x] = 0.5 * c * e2 * s * k
        return carry

    lax.fori_loop(0, courant.shape[0], layer, 0)

    rows, columns = index.shape
    pieces = [(r, y) for r in range(0, rows, 8) for y in range(0, columns, 128)]
    low = []
    high = []
    for r, y in pieces:
        i = index[r : r + 8, y : y + 128]
        low.append(i & 127)
        high.append(i >> 7)

    def at_time(t, carry):
        found = [jnp.zeros((8, 128), jnp.float32) for _ in pieces]
        for h in range(traces.shape[1]):
            row = jnp.broadcast_to(traces[t, h : h + 1], (8, 128))
            for p in range(len(pieces)):
                value = jnp.take_along_axis(row, low[p], axis=1, mode="promise_in_bounds")
                found[p] = jnp.where(high[p] == h, value, found[p])
        for (r, y), value in zip(pieces, found):
            for i in range(8):
                inject[t, r + i, :, y : y + 128] = value[i : i + 1]
        return carry

    lax.fori_loop(0, traces.shape[0], at_time, 0)


def wave_kernel(
    count,
    wave_now, wave_prev, coefs, inject,
    wave_out, snaps,
    even, odd, send, halo, own, zero,
    local_sem, send_sem, recv_sem, snap_send, snap_recv, snap_local, zero_sem,
):
    width = wave_now.shape[1]
    shot = lax.axis_index("shot")
    me = lax.axis_index("gx")
    has_left = me > 0
    has_right = me < count - 1
    sides = ((0, has_left, me - 1), (1, has_right, me + 1))

    barrier = pltpu.get_barrier_semaphore()
    for _, there, other in sides:
        @pl.when(there)
        def _():
            pl.semaphore_signal(barrier, inc=1, device_id=(shot, other), device_id_type=MESH)

    load_now = pltpu.make_async_copy(wave_now, even.at[:, pl.ds(2, width)], local_sem.at[0])
    load_prev = pltpu.make_async_copy(wave_prev, odd.at[:, pl.ds(2, width)], local_sem.at[1])
    load_now.start()
    load_prev.start()

    for side, there, _ in sides:
        @pl.when(jnp.logical_not(there))
        def _():
            zero[...] = jnp.zeros(zero.shape, zero.dtype)
            for ref in (even, odd):
                ref[:, pl.ds(side * (width + 2), 2)] = jnp.zeros((2, 2) + ref.shape[2:], ref.dtype)

    def edge_copies():
        found = []
        for side, there, _ in sides:
            for b in range(SNAPS):
                for f in range(2):
                    found.append((there, pltpu.make_async_copy(
                        zero, snaps.at[b, f, pl.ds(side * 2 * width, width)],
                        zero_sem.at[side, b, f])))
        return found

    for there, copy in edge_copies():
        @pl.when(jnp.logical_not(there))
        def _():
            copy.start()

    pl.semaphore_wait(barrier, has_left.astype(jnp.int32) + has_right.astype(jnp.int32))

    def halo_copy(t, side, other):
        return pltpu.make_async_remote_copy(
            src_ref=send.at[t, side],
            dst_ref=halo.at[t, 1 - side],
            send_sem=send_sem.at[t, side],
            recv_sem=recv_sem.at[t, 1 - side],
            device_id=(shot, other),
            device_id_type=MESH,
        )

    def halo_arrival(t, side, other):
        return pltpu.make_async_remote_copy(
            src_ref=send.at[t, side],
            dst_ref=halo.at[t, side],
            send_sem=send_sem.at[t, side],
            recv_sem=recv_sem.at[t, side],
            device_id=(shot, other),
            device_id_type=MESH,
        )

    def snap_copy(b, side, other, place):
        return pltpu.make_async_remote_copy(
            src_ref=own.at[b],
            dst_ref=snaps.at[b, :, pl.ds(place * 2 * width, width)],
            send_sem=snap_send.at[b, side],
            recv_sem=snap_recv.at[b, place],
            device_id=(shot, other),
            device_id_type=MESH,
        )

    def own_copy(b):
        return pltpu.make_async_copy(own.at[b], snaps.at[b, :, pl.ds(width, width)], snap_local.at[b])

    def send_edges(t, ref):
        for side, there, other in sides:
            @pl.when(there)
            def _():
                send[t, side] = ref[:, pl.ds(2 + side * (width - 2), 2)].astype(jnp.bfloat16)
                halo_copy(t, side, other).start()

    depth, cross = wave_now.shape[2:]
    z = lax.broadcasted_iota(jnp.int32, (depth, cross), 0)
    y = lax.broadcasted_iota(jnp.int32, (depth, cross), 1)

    def shift_z(u, move):
        moved = pltpu.roll(u, (-move) % depth, 0)
        inside = (z < depth - move) if move > 0 else (z >= -move)
        return jnp.where(inside, moved, 0.0)

    def shift_y(u, move):
        moved = pltpu.roll(u, (-move) % cross, 1)
        inside = (y < cross - move) if move > 0 else (y >= -move)
        return jnp.where(inside, moved, 0.0)

    def advance(now, prev, t, x):
        centre, cx, cz, cy, cm = (coefs[i, x] for i in range(5))
        row = jnp.broadcast_to(inject[t, x], (depth, cross))
        for f in range(2):
            u = now[f, x + 2]
            before = now[f, x + 1]
            after = now[f, x + 3]
            total = centre * u - prev[f, x + 2]
            total += cx * ((before + after) - (now[f, x] + now[f, x + 4]) * 0.0625)
            far_z = shift_z(u, 2) + shift_z(u, -2)
            total += cz * ((shift_z(u, 1) + shift_z(u, -1)) - far_z * 0.0625)
            far_y = shift_y(u, 2) + shift_y(u, -2)
            total += cy * ((shift_y(u, 1) + shift_y(u, -1)) - far_y * 0.0625)
            across = after - before
            total += cm * (shift_z(across, 1) - shift_z(across, -1))
            if f == 1:
                total += jnp.where(z == 0, row, 0.0)
            prev[f, x + 2] = total

    load_now.wait()
    send_edges(0, even)
    load_prev.wait()

    def block(b, carry):
        for j in range(SUB):
            now, prev = (even, odd) if j % 2 == 0 else (odd, even)
            t = b * SUB + j
            if j == 0:
                own[b] = now[:, pl.ds(2, width)].astype(jnp.bfloat16)
                own_copy(b).start()
                for side, there, other in sides:
                    @pl.when(there)
                    def _():
                        snap_copy(b, side, other, 1 - side).start()

            def inner(x, c):
                advance(now, prev, t, x)
                return c

            lax.fori_loop(2, width - 2, inner, 0)
            for side, there, other in sides:
                @pl.when(there)
                def _():
                    halo_arrival(t, side, other).wait_recv()
                    now[:, pl.ds(side * (width + 2), 2)] = halo[t, side].astype(jnp.float32)

                def edge(i, c):
                    advance(now, prev, t, side * (width - 2) + i)
                    return c

                lax.fori_loop(0, 2, edge, 0)

            if j < SUB - 1:
                send_edges(t + 1, prev)
            else:
                @pl.when(b < SNAPS - 1)
                def _():
                    send_edges(t + 1, prev)
        return carry

    lax.fori_loop(0, SNAPS, block, 0)

    store = pltpu.make_async_copy(even.at[:, pl.ds(2, width)], wave_out, local_sem.at[0])
    store.start()
    for side, there, other in sides:
        @pl.when(there)
        def _():
            def drain(t, c):
                halo_copy(t, side, other).wait_send()
                return c

            lax.fori_loop(0, STEPS, drain, 0)
            for b in range(SNAPS):
                snap_copy(b, side, other, 1 - side).wait_send()
                snap_copy(b, side, other, side).wait_recv()
    for there, copy in edge_copies():
        @pl.when(jnp.logical_not(there))
        def _():
            copy.wait()
    for b in range(SNAPS):
        own_copy(b).wait()
    store.wait()


def correlate_kernel(lags, snaps, image):
    h = lags[pl.program_id(0)] - HALF
    width = image.shape[1]
    for x in range(width):
        terms = [snaps[b, 0, HALF - h + x] * snaps[b, 1, HALF + h + x] for b in range(SNAPS)]
        image[0, x] = (terms[0] + terms[1]) + (terms[2] + terms[3])


def body(count, wave_now, wave_prev, courant, epsilon, tilt, trace_index, traces, lag_list):
    _, width, depth, cross = wave_now.shape
    vmem = pl.BlockSpec(memory_space=pltpu.VMEM)
    whole = pl.BlockSpec(memory_space=pl.ANY)
    coefs, inject = pl.pallas_call(
        prep_kernel,
        out_shape=(
            jax.ShapeDtypeStruct((5, width, depth, cross), jnp.float32),
            jax.ShapeDtypeStruct((STEPS, width, 1, cross), jnp.float32),
        ),
        in_specs=[vmem] * 5,
        out_specs=(vmem, vmem),
        compiler_params=pltpu.CompilerParams(vmem_limit_bytes=LIMIT),
    )(courant, epsilon, tilt, trace_index, traces.reshape(STEPS, -1, 128))

    state = pltpu.VMEM((2, width + 4, depth, cross), jnp.float32)
    edges = pltpu.VMEM((STEPS, 2, 2, 2, depth, cross), jnp.bfloat16)
    dma = pltpu.SemaphoreType.DMA
    wave_out, snaps = pl.pallas_call(
        functools.partial(wave_kernel, count),
        out_shape=(
            jax.ShapeDtypeStruct(wave_now.shape, jnp.float32),
            jax.ShapeDtypeStruct((SNAPS, 2, 3 * width, depth, cross), jnp.bfloat16),
        ),
        in_specs=[whole, whole, vmem, vmem],
        out_specs=(whole, whole),
        scratch_shapes=[
            state, state, edges, edges,
            pltpu.VMEM((SNAPS, 2, width, depth, cross), jnp.bfloat16),
            pltpu.VMEM((width, depth, cross), jnp.bfloat16),
            dma((2,)),
            dma((STEPS, 2)),
            dma((STEPS, 2)),
            dma((SNAPS, 2)),
            dma((SNAPS, 2)),
            dma((SNAPS,)),
            dma((2, SNAPS, 2)),
        ],
        compiler_params=pltpu.CompilerParams(
            collective_id=0, has_side_effects=True, vmem_limit_bytes=LIMIT
        ),
    )(wave_now, wave_prev, coefs, inject)

    image_out = pl.pallas_call(
        correlate_kernel,
        out_shape=jax.ShapeDtypeStruct((LAGS, width, depth, cross), jnp.bfloat16),
        grid_spec=pltpu.PrefetchScalarGridSpec(
            num_scalar_prefetch=1,
            grid=(LAGS,),
            in_specs=[vmem],
            out_specs=pl.BlockSpec((1, width, depth, cross), lambda k, lags: (k, 0, 0, 0)),
        ),
        compiler_params=pltpu.CompilerParams(vmem_limit_bytes=LIMIT),
    )(lag_list, snaps)
    return (image_out, wave_out)


def solution(mesh):
    placed = (
        P("shot", "gx", None, None),
        P("shot", "gx", None, None),
        P("gx", "shot", None),
        P("gx", "shot", None),
        P("gx", "shot", None),
        P("gx", "shot"),
        P("shot", None),
        P(),
    )
    return jax.shard_map(
        functools.partial(body, mesh.shape["gx"]),
        mesh=mesh,
        in_specs=placed,
        out_specs=(P("shot", "gx", None, None), P("shot", "gx", None, None)),
        check_vma=False,
    )
```

time: 326 us -> 89.1 us (0.27)
  starting transfers between devices: 111 us -> 0 us
  other arithmetic: 108 us -> 0 us
  Pallas kernels: 0 us -> 78.2 us
  waiting for transfers between devices: 53.9 us -> 0 us
  local copies, waits for them, and re-layouts: 46.2 us -> 9.26 us
    ppermute x40 -> x0, starting transfers between devices: 111 us -> none  [the longest x20 70.6 us: with_halo(): lax.ppermute(lax.slice_in_dim(block, block.shape[dim] - width, None, axis...]
    add x37 -> x0, other arithmetic: 89.4 us -> none  [the longest x4 46.5 us: block_pass(): image_sum = image_sum + correlate(extended, slab_width)]
    pallas_call x0 -> x3, Pallas kernels: none -> 78.2 us  [the longest x1 59.9 us: body(): pl.pallas_call(functools.partial(wave_kernel, count), out_shape=(jax.Shap...]
    ppermute x40 -> x0, waiting for transfers between devices: 53.9 us -> none  [the longest x20 48.8 us: with_halo(): lax.ppermute(lax.slice_in_dim(block, 0, width, axis=dim), axis, backward)]
    gather x3 -> x0, local copies, waits for them, and re-layouts: 26.9 us -> none  [the longest x2 18.3 us: body(): inject = traces[:, trace_index]]
    while x28 -> x0, local copies, waits for them, and re-layouts: 13.5 us -> none
    concatenate x16 -> x0, other arithmetic: 7.75 us -> none  [with_halo(): block = jnp.concatenate([low, block, high], axis=dim)]
    unnamed x12 -> x18, local copies, waits for them, and re-layouts: 2.26 us -> 9.26 us
  transfers between devices with their start and end apart: 40 -> 0, of which waited for: 16 -> 0; matrix products, arithmetic and copies ran while one was open for 4% -> 0% of each run, Pallas kernels for 0% -> 0%
where the time goes in v1:
time: 89.1 us; the launch traced here: 88.1 us
  Pallas kernels  78.2 us (88%)
  local copies, waits for them, and re-layouts  9.26 us (10%)
    pallas_call x1, Pallas kernels, body(): pl.pallas_call(functools.partial(wave_kernel, count), out_shape=(jax.Shap...  59.9 us
    pallas_call x1, Pallas kernels, body(): pl.pallas_call(correlate_kernel, out_shape=jax.ShapeDtypeStruct((LAGS, wi...  12.8 us
    unnamed x18, local copies, waits for them, and re-layouts  9.26 us
    pallas_call x1, Pallas kernels, body(): pl.pallas_call(prep_kernel, out_shape=(jax.ShapeDtypeStruct((5, width, de...  5.46 us

profile of v1, /device:TPU:1, one launch (start us, length us, event | category | flops | bytes accessed | tf_op | source)
XLA Modules:
  0.0 88.1 jit_solution(13192730927093071739)
XLA Ops:
  0.6 0.0 copy-start.7
  0.6 0.9 %copy.10 = f32[2,8,16,128]{3,2,1,0:T(8,128)S(1)} copy(f32[2,8,16,128]{3,1,2,0:T(8,128)} %bitcast.3) | data formatting | bytes 262144
  1.6 0.0 copy-start.3
  1.6 0.9 %copy-done.3 = f32[16,16,256]{2,1,0:T(8,128)S(1)} copy-done((f32[16,16,256]{2,1,0:T(8,128)S(1)}, f32[16,16,256]{2,1,0:T(8,128)}, u32[]{:S(2)}) %copy-start.3) | copy-done | bytes 262168
  2.5 0.0 copy-start.4
  2.5 0.9 %copy-done.4 = f32[16,16,256]{2,1,0:T(8,128)S(1)} copy-done((f32[16,16,256]{2,1,0:T(8,128)S(1)}, f32[16,16,256]{2,1,0:T(8,128)}, u32[]{:S(2)}) %copy-start.4) | copy-done | bytes 262168
  3.5 0.0 copy-start.5
  3.5 0.9 %copy-done.5 = f32[16,16,256]{2,1,0:T(8,128)S(1)} copy-done((f32[16,16,256]{2,1,0:T(8,128)S(1)}, f32[16,16,256]{2,1,0:T(8,128)}, u32[]{:S(2)}) %copy-start.5) | copy-done | bytes 262168
  4.4 0.0 copy-start.6
  4.4 0.7 copy-done.6
  5.2 5.5 %shard_map.95 = (f32[5,16,16,256]{3,2,1,0:T(8,128)S(1)}, f32[16,16,1,256]{3,2,1,0:T(1,128)S(1)}) custom-call(f32[16,16,256]{2,1,0:T(8,128)S(1)} %copy-done.3, f32[16,16,256]{2,1,0:T(8,128)S(1)} %copy-done.4, f32[16,16,256]{2,1,0:T(8,128)S(1)} %copy-done.5, s32[16,256]{1,0:T(8,128)S(1)} %copy-done.6, f32[16,16,128]{2,1,0:T(8,128)S(1)} %bitcast.2), custom_call_target="tpu_custom_call" | custom-call | tf_op jit(solution)/shard_map/pallas_call | solution.py:259
  10.6 0.0 copy-start.1
  10.6 1.0 %copy-done.1 = f32[2,16,16,256]{3,2,1,0:T(8,128)S(1)} copy-done((f32[2,16,16,256]{3,2,1,0:T(8,128)S(1)}, f32[2,16,16,256]{3,2,1,0:T(8,128)}, u32[]{:S(2)}) %copy-start.1) | copy-done | bytes 524312
  11.7 0.0 copy-start.2
  11.7 1.0 %copy-done.2 = f32[2,16,16,256]{3,2,1,0:T(8,128)S(1)} copy-done((f32[2,16,16,256]{3,2,1,0:T(8,128)S(1)}, f32[2,16,16,256]{3,2,1,0:T(8,128)}, u32[]{:S(2)}) %copy-start.2) | copy-done | bytes 524312
  12.7 59.9 %shard_map.96 = (f32[2,16,16,256]{3,2,1,0:T(8,128)S(1)}, bf16[4,2,48,16,256]{4,3,2,1,0:T(8,128)(2,1)}) custom-call(f32[2,16,16,256]{3,2,1,0:T(8,128)S(1)} %copy-done.1, f32[2,16,16,256]{3,2,1,0:T(8,128)S(1)} %copy-done.2, f32[5,16,16,256]{3,2,1,0:T(8,128)S(1)} %get-tuple-element.6.coefs, f32[16,16,1,256]{3,2,1,0:T(1,128)S(1)} %get-tuple-element.7.inject), custom_call_target="tpu_custom_call" | custom-call | tf_op jit(solution)/shard_map/pallas_call | solution.py:273
  72.7 0.0 copy-done.7
  72.7 0.0 copy-start
  72.7 1.9 %copy-done = bf16[4,2,48,16,256]{4,3,2,1,0:T(8,128)(2,1)S(1)} copy-done((bf16[4,2,48,16,256]{4,3,2,1,0:T(8,128)(2,1)S(1)}, bf16[4,2,48,16,256]{4,3,2,1,0:T(8,128)(2,1)}, u32[]{:S(2)}) %copy-start) | copy-done | bytes 3145752
  74.6 12.8 %shard_map.97 = bf16[33,16,16,256]{3,2,1,0:T(8,128)(2,1)} custom-call(s32[33]{0:T(128)S(1)} %copy-done.7, bf16[4,2,48,16,256]{4,3,2,1,0:T(8,128)(2,1)S(1)} %copy-done), custom_call_target="tpu_custom_call" | custom-call | tf_op jit(solution)/shard_map/pallas_call | solution.py:298
  87.3 0.8 copy.12
Async XLA Ops:
  0.6 72.0 %copy-start.7 = (s32[33]{0:T(128)S(1)}, s32[33]{0:T(128)}, u32[]{:S(2)}) copy-start(s32[33]{0:T(128)} %lags.1) | copy-start | bytes 400
  1.6 1.0 %copy-start.3 = (f32[16,16,256]{2,1,0:T(8,128)S(1)}, f32[16,16,256]{2,1,0:T(8,128)}, u32[]{:S(2)}) copy-start(f32[16,16,256]{2,1,0:T(8,128)} %courant.1) | copy-start | bytes 786436
  2.5 0.9 %copy-start.4 = (f32[16,16,256]{2,1,0:T(8,128)S(1)}, f32[16,16,256]{2,1,0:T(8,128)}, u32[]{:S(2)}) copy-start(f32[16,16,256]{2,1,0:T(8,128)} %epsilon.1) | copy-start | bytes 786436
  3.5 0.9 %copy-start.5 = (f32[16,16,256]{2,1,0:T(8,128)S(1)}, f32[16,16,256]{2,1,0:T(8,128)}, u32[]{:S(2)}) copy-start(f32[16,16,256]{2,1,0:T(8,128)} %tilt.1) | copy-start | bytes 786436
  4.4 0.7 copy-start.6
  10.6 1.0 %copy-start.1 = (f32[2,16,16,256]{3,2,1,0:T(8,128)S(1)}, f32[2,16,16,256]{3,2,1,0:T(8,128)}, u32[]{:S(2)}) copy-start(f32[2,16,16,256]{3,2,1,0:T(8,128)} %wave_now.1) | copy-start | bytes 1572868
  11.7 1.0 %copy-start.2 = (f32[2,16,16,256]{3,2,1,0:T(8,128)S(1)}, f32[2,16,16,256]{3,2,1,0:T(8,128)}, u32[]{:S(2)}) copy-start(f32[2,16,16,256]{3,2,1,0:T(8,128)} %wave_prev.1) | copy-start | bytes 1572868
  72.7 1.9 %copy-start = (bf16[4,2,48,16,256]{4,3,2,1,0:T(8,128)(2,1)S(1)}, bf16[4,2,48,16,256]{4,3,2,1,0:T(8,128)(2,1)}, u32[]{:S(2)}) copy-start(bf16[4,2,48,16,256]{4,3,2,1,0:T(8,128)(2,1)} %get-tuple-element.8.snaps) | copy-start | bytes 9437188

commit v2 on v1

--- a/solution.py
+++ b/solution.py
@@ -7,11 +7,13 @@
 from jax.experimental.pallas import tpu as pltpu
 from jax.sharding import PartitionSpec as P
 
-SUB = 4
 SNAPS = 4
 STEPS = 16
 LAGS = 33
 HALF = 16
+GROUP = 11
+PAIRS = STEPS // 2
+DEEP = 4
 MESH = pl.DeviceIdType.MESH
 LIMIT = 48 * 1024 * 1024
 
@@ -59,10 +61,10 @@
 
 def wave_kernel(
     count,
-    wave_now, wave_prev, coefs, inject,
+    wave_now, wave_prev, coefs_here, inject_here,
     wave_out, snaps,
-    even, odd, send, halo, own, zero,
-    local_sem, send_sem, recv_sem, snap_send, snap_recv, snap_local, zero_sem,
+    even, odd, coefs, inject, send, halo, own, zero,
+    local_sem, first_send, first_recv, send_sem, recv_sem, snap_send, snap_recv, snap_local, zero_sem,
 ):
     width = wave_now.shape[1]
     shot = lax.axis_index("shot")
@@ -77,17 +79,39 @@
         def _():
             pl.semaphore_signal(barrier, inc=1, device_id=(shot, other), device_id_type=MESH)
 
-    load_now = pltpu.make_async_copy(wave_now, even.at[:, pl.ds(2, width)], local_sem.at[0])
-    load_prev = pltpu.make_async_copy(wave_prev, odd.at[:, pl.ds(2, width)], local_sem.at[1])
-    load_now.start()
-    load_prev.start()
+    loads = [
+        pltpu.make_async_copy(source, target.at[:, pl.ds(pad, width)], local_sem.at[i])
+        for i, (source, target, pad) in enumerate((
+            (wave_now, even, DEEP), (wave_prev, odd, DEEP),
+            (coefs_here, coefs, 2), (inject_here, inject, 2),
+        ))
+    ]
+    for load in loads:
+        load.start()
+
+    def first_copies(side, other, place):
+        found = []
+        for i, (source, target, pad) in enumerate((
+            (wave_prev, odd, DEEP), (coefs_here, coefs, 2), (inject_here, inject, 2),
+        )):
+            start = pad - 2 if place == 0 else pad + width
+            found.append(pltpu.make_async_remote_copy(
+                src_ref=source.at[:, pl.ds(side * (width - 2), 2)],
+                dst_ref=target.at[:, pl.ds(start, 2)],
+                send_sem=first_send.at[i, side],
+                recv_sem=first_recv.at[i, place],
+                device_id=(shot, other),
+                device_id_type=MESH,
+            ))
+        return found
 
     for side, there, _ in sides:
         @pl.when(jnp.logical_not(there))
         def _():
             zero[...] = jnp.zeros(zero.shape, zero.dtype)
             for ref in (even, odd):
-                ref[:, pl.ds(side * (width + 2), 2)] = jnp.zeros((2, 2) + ref.shape[2:], ref.dtype)
+                ref[:, pl.ds(side * (width + DEEP), DEEP)] = jnp.zeros(
+                    (2, DEEP) + ref.shape[2:], ref.dtype)
 
     def edge_copies():
         found = []
@@ -143,7 +167,7 @@
         for side, there, other in sides:
             @pl.when(there)
             def _():
-                send[t, side] = ref[:, pl.ds(2 + side * (width - 2), 2)].astype(jnp.bfloat16)
+                send[t, side] = ref[:, pl.ds(DEEP + side * (width - DEEP), DEEP)].astype(jnp.bfloat16)
                 halo_copy(t, side, other).start()
 
     depth, cross = wave_now.shape[2:]
@@ -161,14 +185,14 @@
         return jnp.where(inside, moved, 0.0)
 
     def advance(now, prev, t, x):
-        centre, cx, cz, cy, cm = (coefs[i, x] for i in range(5))
-        row = jnp.broadcast_to(inject[t, x], (depth, cross))
+        centre, cx, cz, cy, cm = (coefs[i, x + 2] for i in range(5))
+        row = jnp.broadcast_to(inject[t, x + 2], (depth, cross))
         for f in range(2):
-            u = now[f, x + 2]
-            before = now[f, x + 1]
-            after = now[f, x + 3]
-            total = centre * u - prev[f, x + 2]
-            total += cx * ((before + after) - (now[f, x] + now[f, x + 4]) * 0.0625)
+            u = now[f, x + 4]
+            before = now[f, x + 3]
+            after = now[f, x + 5]
+            total = centre * u - prev[f, x + 4]
+            total += cx * ((before + after) - (now[f, x + 2] + now[f, x + 6]) * 0.0625)
             far_z = shift_z(u, 2) + shift_z(u, -2)
             total += cz * ((shift_z(u, 1) + shift_z(u, -1)) - far_z * 0.0625)
             far_y = shift_y(u, 2) + shift_y(u, -2)
@@ -177,52 +201,66 @@
             total += cm * (shift_z(across, 1) - shift_z(across, -1))
             if f == 1:
                 total += jnp.where(z == 0, row, 0.0)
-            prev[f, x + 2] = total
-
-    load_now.wait()
+            prev[f, x + 4] = total
+
+    loads[0].wait()
     send_edges(0, even)
-    load_prev.wait()
-
-    def block(b, carry):
-        for j in range(SUB):
-            now, prev = (even, odd) if j % 2 == 0 else (odd, even)
-            t = b * SUB + j
-            if j == 0:
-                own[b] = now[:, pl.ds(2, width)].astype(jnp.bfloat16)
-                own_copy(b).start()
-                for side, there, other in sides:
-                    @pl.when(there)
-                    def _():
-                        snap_copy(b, side, other, 1 - side).start()
-
-            def inner(x, c):
-                advance(now, prev, t, x)
-                return c
-
-            lax.fori_loop(2, width - 2, inner, 0)
+    for side, there, other in sides:
+        @pl.when(there)
+        def _():
+            for copy in first_copies(side, other, 1 - side):
+                copy.start()
+    for load in loads[1:]:
+        load.wait()
+
+    def run(now, prev, t, first, number, unroll):
+        def one(i, c):
+            advance(now, prev, t, first + i)
+            return c
+
+        lax.fori_loop(0, number, one, 0, unroll=unroll)
+
+    def pair(p, carry):
+        t = 2 * p
+
+        @pl.when(p % 2 == 0)
+        def _():
+            b = p // 2
+            own[b] = even[:, pl.ds(DEEP, width)].astype(jnp.bfloat16)
+            own_copy(b).start()
             for side, there, other in sides:
                 @pl.when(there)
                 def _():
-                    halo_arrival(t, side, other).wait_recv()
-                    now[:, pl.ds(side * (width + 2), 2)] = halo[t, side].astype(jnp.float32)
-
-                def edge(i, c):
-                    advance(now, prev, t, side * (width - 2) + i)
-                    return c
-
-                lax.fori_loop(0, 2, edge, 0)
-
-            if j < SUB - 1:
-                send_edges(t + 1, prev)
-            else:
-                @pl.when(b < SNAPS - 1)
+                    snap_copy(b, side, other, 1 - side).start()
+
+        run(even, odd, t, 2, width - 4, 4)
+        run(odd, even, t + 1, 4, width - 8, 4)
+        for side, there, other in sides:
+            @pl.when(there)
+            def _():
+                halo_arrival(p, side, other).wait_recv()
+                even[:, pl.ds(side * (width + DEEP), DEEP)] = halo[p, side].astype(jnp.float32)
+
+                @pl.when(p == 0)
                 def _():
-                    send_edges(t + 1, prev)
+                    for copy in first_copies(side, other, side):
+                        copy.wait_recv()
+
+                run(even, odd, t, side * (width + 2) - 2, 2, 2)
+        for side, _, _ in sides:
+            run(even, odd, t, side * (width - 2), 2, 2)
+        for side, _, _ in sides:
+            run(odd, even, t + 1, side * (width - 4), 4, 4)
+
+        @pl.when(p < PAIRS - 1)
+        def _():
+            send_edges(p + 1, even)
+
         return carry
 
-    lax.fori_loop(0, SNAPS, block, 0)
-
-    store = pltpu.make_async_copy(even.at[:, pl.ds(2, width)], wave_out, local_sem.at[0])
+    lax.fori_loop(0, PAIRS, pair, 0)
+
+    store = pltpu.make_async_copy(even.at[:, pl.ds(DEEP, width)], wave_out, local_sem.at[0])
     store.start()
     for side, there, other in sides:
         @pl.when(there)
@@ -231,7 +269,9 @@
                 halo_copy(t, side, other).wait_send()
                 return c
 
-            lax.fori_loop(0, STEPS, drain, 0)
+            lax.fori_loop(0, PAIRS, drain, 0)
+            for copy in first_copies(side, other, 1 - side):
+                copy.wait_send()
             for b in range(SNAPS):
                 snap_copy(b, side, other, 1 - side).wait_send()
                 snap_copy(b, side, other, side).wait_recv()
@@ -245,11 +285,16 @@
 
 
 def correlate_kernel(lags, snaps, image):
-    h = lags[pl.program_id(0)] - HALF
-    width = image.shape[1]
-    for x in range(width):
-        terms = [snaps[b, 0, HALF - h + x] * snaps[b, 1, HALF + h + x] for b in range(SNAPS)]
-        image[0, x] = (terms[0] + terms[1]) + (terms[2] + terms[3])
+    group, width = image.shape[:2]
+
+    def one(k, carry):
+        h = lags[pl.program_id(0) * group + k] - HALF
+        for x in range(width):
+            terms = [snaps[b, 0, HALF - h + x] * snaps[b, 1, HALF + h + x] for b in range(SNAPS)]
+            image[k, x] = (terms[0] + terms[1]) + (terms[2] + terms[3])
+        return carry
+
+    lax.fori_loop(0, group, one, 0)
 
 
 def body(count, wave_now, wave_prev, courant, epsilon, tilt, trace_index, traces, lag_list):
@@ -267,8 +312,8 @@
         compiler_params=pltpu.CompilerParams(vmem_limit_bytes=LIMIT),
     )(courant, epsilon, tilt, trace_index, traces.reshape(STEPS, -1, 128))
 
-    state = pltpu.VMEM((2, width + 4, depth, cross), jnp.float32)
-    edges = pltpu.VMEM((STEPS, 2, 2, 2, depth, cross), jnp.bfloat16)
+    state = pltpu.VMEM((2, width + 2 * DEEP, depth, cross), jnp.float32)
+    edges = pltpu.VMEM((PAIRS, 2, 2, DEEP, depth, cross), jnp.bfloat16)
     dma = pltpu.SemaphoreType.DMA
     wave_out, snaps = pl.pallas_call(
         functools.partial(wave_kernel, count),
@@ -276,15 +321,20 @@
             jax.ShapeDtypeStruct(wave_now.shape, jnp.float32),
             jax.ShapeDtypeStruct((SNAPS, 2, 3 * width, depth, cross), jnp.bfloat16),
         ),
-        in_specs=[whole, whole, vmem, vmem],
+        in_specs=[whole] * 4,
         out_specs=(whole, whole),
         scratch_shapes=[
-            state, state, edges, edges,
+            state, state,
+            pltpu.VMEM((5, width + 4, depth, cross), jnp.float32),
+            pltpu.VMEM((STEPS, width + 4, 1, cross), jnp.float32),
+            edges, edges,
             pltpu.VMEM((SNAPS, 2, width, depth, cross), jnp.bfloat16),
             pltpu.VMEM((width, depth, cross), jnp.bfloat16),
-            dma((2,)),
-            dma((STEPS, 2)),
-            dma((STEPS, 2)),
+            dma((4,)),
+            dma((3, 2)),
+            dma((3, 2)),
+            dma((PAIRS, 2)),
+            dma((PAIRS, 2)),
             dma((SNAPS, 2)),
             dma((SNAPS, 2)),
             dma((SNAPS,)),
@@ -300,9 +350,9 @@
         out_shape=jax.ShapeDtypeStruct((LAGS, width, depth, cross), jnp.bfloat16),
         grid_spec=pltpu.PrefetchScalarGridSpec(
             num_scalar_prefetch=1,
-            grid=(LAGS,),
+            grid=(LAGS // GROUP,),
             in_specs=[vmem],
-            out_specs=pl.BlockSpec((1, width, depth, cross), lambda k, lags: (k, 0, 0, 0)),
+            out_specs=pl.BlockSpec((GROUP, width, depth, cross), lambda k, lags: (k, 0, 0, 0)),
         ),
         compiler_params=pltpu.CompilerParams(vmem_limit_bytes=LIMIT),
     )(lag_list, snaps)

time: 89.1 us -> 70 us (0.79)
  Pallas kernels: 78.2 us -> 59.6 us
    pallas_call x1, Pallas kernels: 59.9 us -> 49.9 us  [body(): pl.pallas_call(functools.partial(wave_kernel, count), out_shape=(jax.Shap...]
    pallas_call x1, Pallas kernels: 12.8 us -> 4.21 us  [body(): pl.pallas_call(correlate_kernel, out_shape=jax.ShapeDtypeStruct((LAGS, wi...]
where the time goes in v2:
time: 70 us; the launch traced here: 69.6 us
  Pallas kernels  59.6 us (85%)
  local copies, waits for them, and re-layouts  9.26 us (13%)
    pallas_call x1, Pallas kernels, body(): pl.pallas_call(functools.partial(wave_kernel, count), out_shape=(jax.Shap...  49.9 us
    unnamed x18, local copies, waits for them, and re-layouts  9.26 us
    pallas_call x1, Pallas kernels, body(): pl.pallas_call(prep_kernel, out_shape=(jax.ShapeDtypeStruct((5, width, de...  5.46 us
    pallas_call x1, Pallas kernels, body(): pl.pallas_call(correlate_kernel, out_shape=jax.ShapeDtypeStruct((LAGS, wi...  4.21 us

profile of v2, /device:TPU:1, one launch (start us, length us, event | category | flops | bytes accessed | tf_op | source)
XLA Modules:
  0.0 69.6 jit_solution(9672548434367941886)
XLA Ops:
  0.6 0.0 copy-start.7
  0.6 0.9 %copy.10 = f32[2,8,16,128]{3,2,1,0:T(8,128)S(1)} copy(f32[2,8,16,128]{3,1,2,0:T(8,128)} %bitcast.3) | data formatting | bytes 262144
  1.6 0.0 copy-start.3
  1.6 0.9 %copy-done.3 = f32[16,16,256]{2,1,0:T(8,128)S(1)} copy-done((f32[16,16,256]{2,1,0:T(8,128)S(1)}, f32[16,16,256]{2,1,0:T(8,128)}, u32[]{:S(2)}) %copy-start.3) | copy-done | bytes 262168
  2.5 0.0 copy-start.4
  2.5 0.9 %copy-done.4 = f32[16,16,256]{2,1,0:T(8,128)S(1)} copy-done((f32[16,16,256]{2,1,0:T(8,128)S(1)}, f32[16,16,256]{2,1,0:T(8,128)}, u32[]{:S(2)}) %copy-start.4) | copy-done | bytes 262168
  3.5 0.0 copy-start.5
  3.5 0.9 %copy-done.5 = f32[16,16,256]{2,1,0:T(8,128)S(1)} copy-done((f32[16,16,256]{2,1,0:T(8,128)S(1)}, f32[16,16,256]{2,1,0:T(8,128)}, u32[]{:S(2)}) %copy-start.5) | copy-done | bytes 262168
  4.4 0.0 copy-start.6
  4.4 0.7 %copy-done.6 = s32[16,256]{1,0:T(8,128)S(1)} copy-done((s32[16,256]{1,0:T(8,128)S(1)}, s32[16,256]{1,0:T(8,128)}, u32[]{:S(2)}) %copy-start.6) | copy-done | bytes 16408
  5.2 5.5 %shard_map.95 = (f32[5,16,16,256]{3,2,1,0:T(8,128)S(1)}, f32[16,16,1,256]{3,2,1,0:T(1,128)S(1)}) custom-call(f32[16,16,256]{2,1,0:T(8,128)S(1)} %copy-done.3, f32[16,16,256]{2,1,0:T(8,128)S(1)} %copy-done.4, f32[16,16,256]{2,1,0:T(8,128)S(1)} %copy-done.5, s32[16,256]{1,0:T(8,128)S(1)} %copy-done.6, f32[16,16,128]{2,1,0:T(8,128)S(1)} %bitcast.2), custom_call_target="tpu_custom_call" | custom-call | tf_op jit(solution)/shard_map/pallas_call | solution.py:304
  10.6 0.0 copy-start.1
  10.6 1.0 %copy-done.1 = f32[2,16,16,256]{3,2,1,0:T(8,128)S(1)} copy-done((f32[2,16,16,256]{3,2,1,0:T(8,128)S(1)}, f32[2,16,16,256]{3,2,1,0:T(8,128)}, u32[]{:S(2)}) %copy-start.1) | copy-done | bytes 524312
  11.7 0.0 copy-start.2
  11.7 1.0 %copy-done.2 = f32[2,16,16,256]{3,2,1,0:T(8,128)S(1)} copy-done((f32[2,16,16,256]{3,2,1,0:T(8,128)S(1)}, f32[2,16,16,256]{3,2,1,0:T(8,128)}, u32[]{:S(2)}) %copy-start.2) | copy-done | bytes 524312
  12.7 49.9 %shard_map.96 = (f32[2,16,16,256]{3,2,1,0:T(8,128)S(1)}, bf16[4,2,48,16,256]{4,3,2,1,0:T(8,128)(2,1)}) custom-call(f32[2,16,16,256]{3,2,1,0:T(8,128)S(1)} %copy-done.1, f32[2,16,16,256]{3,2,1,0:T(8,128)S(1)} %copy-done.2, f32[5,16,16,256]{3,2,1,0:T(8,128)S(1)} %get-tuple-element.6.coefs_here, f32[16,16,1,256]{3,2,1,0:T(1,128)S(1)} %get-tuple-element.7.inject_here), custom_call_target="tpu_custom_call" | custom-call | tf_op jit(solution)/shard_map/pallas_call | solution.py:318
  62.7 0.0 copy-done.7
  62.7 0.0 copy-start
  62.7 1.9 %copy-done = bf16[4,2,48,16,256]{4,3,2,1,0:T(8,128)(2,1)S(1)} copy-done((bf16[4,2,48,16,256]{4,3,2,1,0:T(8,128)(2,1)S(1)}, bf16[4,2,48,16,256]{4,3,2,1,0:T(8,128)(2,1)}, u32[]{:S(2)}) %copy-start) | copy-done | bytes 3145752
  64.6 4.2 %shard_map.97 = bf16[33,16,16,256]{3,2,1,0:T(8,128)(2,1)} custom-call(s32[33]{0:T(128)S(1)} %copy-done.7, bf16[4,2,48,16,256]{4,3,2,1,0:T(8,128)(2,1)S(1)} %copy-done), custom_call_target="tpu_custom_call" | custom-call | tf_op jit(solution)/shard_map/pallas_call | solution.py:348
  68.8 0.8 %copy.12 = f32[2,16,16,256]{3,2,1,0:T(8,128)} copy(f32[2,16,16,256]{3,2,1,0:T(8,128)S(1)} %get-tuple-element.13) | data formatting | bytes 1048576
Async XLA Ops:
  0.6 62.0 %copy-start.7 = (s32[33]{0:T(128)S(1)}, s32[33]{0:T(128)}, u32[]{:S(2)}) copy-start(s32[33]{0:T(128)} %lags.1) | copy-start | bytes 400
  1.6 1.0 %copy-start.3 = (f32[16,16,256]{2,1,0:T(8,128)S(1)}, f32[16,16,256]{2,1,0:T(8,128)}, u32[]{:S(2)}) copy-start(f32[16,16,256]{2,1,0:T(8,128)} %courant.1) | copy-start | bytes 786436
  2.5 0.9 %copy-start.4 = (f32[16,16,256]{2,1,0:T(8,128)S(1)}, f32[16,16,256]{2,1,0:T(8,128)}, u32[]{:S(2)}) copy-start(f32[16,16,256]{2,1,0:T(8,128)} %epsilon.1) | copy-start | bytes 786436
  3.5 0.9 %copy-start.5 = (f32[16,16,256]{2,1,0:T(8,128)S(1)}, f32[16,16,256]{2,1,0:T(8,128)}, u32[]{:S(2)}) copy-start(f32[16,16,256]{2,1,0:T(8,128)} %tilt.1) | copy-start | bytes 786436
  4.4 0.7 %copy-start.6 = (s32[16,256]{1,0:T(8,128)S(1)}, s32[16,256]{1,0:T(8,128)}, u32[]{:S(2)}) copy-start(s32[16,256]{1,0:T(8,128)} %index.1) | copy-start | bytes 49156
  10.6 1.0 %copy-start.1 = (f32[2,16,16,256]{3,2,1,0:T(8,128)S(1)}, f32[2,16,16,256]{3,2,1,0:T(8,128)}, u32[]{:S(2)}) copy-start(f32[2,16,16,256]{3,2,1,0:T(8,128)} %wave_now.1) | copy-start | bytes 1572868
  11.7 1.0 %copy-start.2 = (f32[2,16,16,256]{3,2,1,0:T(8,128)S(1)}, f32[2,16,16,256]{3,2,1,0:T(8,128)}, u32[]{:S(2)}) copy-start(f32[2,16,16,256]{3,2,1,0:T(8,128)} %wave_prev.1) | copy-start | bytes 1572868
  62.7 1.9 %copy-start = (bf16[4,2,48,16,256]{4,3,2,1,0:T(8,128)(2,1)S(1)}, bf16[4,2,48,16,256]{4,3,2,1,0:T(8,128)(2,1)}, u32[]{:S(2)}) copy-start(bf16[4,2,48,16,256]{4,3,2,1,0:T(8,128)(2,1)} %get-tuple-element.8.snaps) | copy-start | bytes 9437188
